TPU v7x, 32 devices: a whole 2x2x4 slice. The times are simulated.
32 devices in a mesh: groups: 2 (over x), docs: 16 (over z, y, core).
Axes of the slice: x: 2, y: 2, z: 4, core: 2. Of those that a mesh axis runs over, the one named last changes fastest.
Arguments:
- prompt_queries: bfloat16 [4096, 8192], P(('groups', 'docs')), parts along dimension 0, may hold values from -24 to 24
- prompt_keys: bfloat16 [4096, 512], P(('groups', 'docs')), parts along dimension 0, may hold values from -6 to 6
- prompt_values: bfloat16 [4096, 512], P(('groups', 'docs')), parts along dimension 0, may hold values from -6 to 6
- cache_keys: bfloat16 [16384, 512], P(('groups', 'docs')), parts along dimension 0, may hold values from -24 to 24
- cache_values: bfloat16 [16384, 512], P(('groups', 'docs')), parts along dimension 0, may hold values from -6 to 6
- doc_blocks: int32 [16], P('groups'), parts along dimension 0, may hold values from 1 to 63, as said below
- reader_docs: int32 [32], P(('groups', 'docs')), parts along dimension 0, may hold values from 0 to 7, as said below
- reader_offsets: int32 [32], P(('groups', 'docs')), parts along dimension 0, may hold values from 0 to 4095
Outputs:
- attended: bfloat16 [4096, 8192], P(('groups', 'docs')), parts along dimension 0
There are 2 independent parts, one for each index of `groups`. A program takes and returns all parts, laid end to end along the dimension named above; each array names one. Nothing has to cross between parts.
Inputs may be any that keep to these rules, and one draw needn't show every extreme that they name: `doc_blocks`: the lengths sum to 256; the longest is exactly 63. `reader_docs`: reader r's document holds one or more of the blocks r * 16 to (r + 1) * 16 - 1.
All inputs are finite; a program needn't handle non-finite values.
Results may differ from a plain program's by a relative error of at most 0.012.
The roundings to bfloat16 on the way count: a program that leaves them out, or rounds other values in their place, can miss the bound.
Values may be sent and summed in bfloat16 or wider, within the bound.
No kernel may reach another device: no remote copies, remote signals or barrier semaphores. Data moves between devices by JAX's collectives and lax.ppermute only.
A program may use at most 128 MiB of HBM per device.

v0:
```python
import functools
import math

import jax
import jax.numpy as jnp
import numpy as np
from jax import lax
from jax.experimental import pallas as pl
from jax.experimental.pallas import tpu as pltpu
from jax.sharding import PartitionSpec as P

HD = 128
BLK = 32
HALF_KV = 2
F32 = jnp.float32
BF16 = jnp.bfloat16

rope_base = 1000000.0
yarn_factor = 4.0
pretrain_context = 32768.0
beta_fast = 32.0
beta_slow = 1.0
attention_gain = 0.1 * math.log(4.0) + 1.0
score_scale = 1.0 / math.sqrt(HD)
EXP2_SCALE = score_scale * math.log2(math.e)
SAFE_LOG2 = 60.0
masked_score = -1e30
ROW_TILE_HEADS = 4
VMEM = 28 * 1024 * 1024


def yarn_table():
    half = HD // 2

    def correction(turns):
        return (
            HD * math.log(pretrain_context / (turns * 2.0 * math.pi)) / (2.0 * math.log(rope_base))
        )

    lower = max(math.floor(correction(beta_fast)), 0)
    upper = min(math.ceil(correction(beta_slow)), HD - 1)
    span_width = max(upper - lower, 0.001)
    table = []
    for column in range(half):
        base_freq = rope_base ** (-2.0 * column / HD)
        fraction = min(max((column - lower) / span_width, 0.0), 1.0)
        table.append(base_freq * fraction / yarn_factor + base_freq * (1.0 - fraction))
    return np.asarray(table, np.float32).astype(np.float64)


def angle_rows(positions, gain):
    angles = np.asarray(positions, np.float64)[:, None] * yarn_table()[None, :]
    cosine = np.cos(angles) * gain
    sine = np.sin(angles) * gain
    return (
        np.concatenate([cosine, cosine], axis=1).astype(np.float32),
        np.concatenate([-sine, sine], axis=1).astype(np.float32),
    )


COARSE = 64


def cache_kernel(
    doc_blocks,
    doc,
    offset,
    table,
    k_ref,
    v_ref,
    q_all,
    k_all,
    v_all,
    mine_ref,
    theirs_ref,
    message,
):
    me = lax.axis_index("docs").astype(jnp.int32)
    half = lax.rem(me, 2)
    ndoc = doc_blocks.shape[0]
    width = HALF_KV * HD
    step = pl.program_id(0)
    @pl.when(step == 0)
    def _():
        place = 0
        for ref in (q_all, k_all, v_all):
            size = ref.shape[1] // 2
            col = pl.multiple_of((1 - half) * size, HD)
            message[:, place : place + size] = ref[:, pl.ds(col, size)]
            place += size
        at = jnp.clip(offset[0], 0, COARSE * COARSE - 1)
        hi = at // COARSE
        shape = (message.shape[0], HD)
        row = lax.broadcasted_iota(jnp.int32, shape, 0) // 16
        value = jnp.where(row == 0, doc[0], jnp.where(row == 1, hi, at - hi * COARSE))
        message[:, place : place + HD] = value.astype(F32).astype(BF16)

    blocks = k_ref.shape[0] // BLK
    first_block = me * blocks * pl.num_programs(0)
    c2 = table[2 * COARSE : 2 * COARSE + BLK, :]
    s2 = table[2 * COARSE + BLK : 2 * COARSE + 2 * BLK, :]
    for b in range(blocks):
        block = first_block + step * blocks + b

        def find(d, carry):
            start, begin = carry
            end = start + doc_blocks[d]
            return (end, jnp.where(start <= block, start, begin))

        _, begin = lax.fori_loop(0, ndoc, find, (jnp.int32(0), jnp.int32(0)), unroll=True)
        place = jnp.clip(block - begin, 0, COARSE - 1)
        c1 = table[pl.ds(place, 1), :]
        s1 = table[pl.ds(place + COARSE, 1), :]
        cosine = c1 * c2 - s1 * s2
        sine = s1 * c2 + c1 * s2
        rows = pl.ds(b * BLK, BLK)
        for out, which in ((mine_ref, half), (theirs_ref, 1 - half)):
            for j in range(HALF_KV):
                col = pl.multiple_of(which * width + j * HD, HD)
                x = k_ref[rows, pl.ds(col, HD)].astype(F32)
                y = x * cosine + pltpu.roll(x, HD // 2, 1) * sine
                out[rows, pl.ds(j * HD, HD)] = y.astype(BF16)
    for out, which in ((mine_ref, half), (theirs_ref, 1 - half)):
        col = pl.multiple_of(which * width, HD)
        out[:, pl.ds(width, width)] = v_ref[:, pl.ds(col, width)]


def prepare_cache(doc_blocks, doc, offset, table, keys, values, prompt):
    tokens, columns = keys.shape
    rows = prompt[0].shape[0]
    wide = sum(a.shape[1] // 2 for a in prompt) + HD
    steps = 2
    whole = lambda shape: pl.BlockSpec(shape, lambda i, *_: (0, 0))
    part = pl.BlockSpec((tokens // steps, columns), lambda i, *_: (i, 0))
    out = pl.BlockSpec((tokens // steps, columns), lambda i, *_: (i, 0))
    return pl.pallas_call(
        cache_kernel,
        grid_spec=pltpu.PrefetchScalarGridSpec(
            num_scalar_prefetch=3,
            grid=(steps,),
            in_specs=[whole(table.shape), part, part] + [whole(a.shape) for a in prompt],
            out_specs=[out, out, whole((rows, wide))],
        ),
        out_shape=[jax.ShapeDtypeStruct((tokens, columns), BF16)] * 2
        + [jax.ShapeDtypeStruct((rows, wide), BF16)],
        cost_estimate=pl.CostEstimate(flops=4000000, bytes_accessed=4 << 20, transcendentals=0),
        name="prepare_cache",
    )(doc_blocks, doc, offset, table, keys, values, *prompt)


def scores_of(q, k):
    return lax.dot_general(q, k, (((1,), (1,)), ((), ())), preferred_element_type=F32)


def square_bound(x):
    sums = jnp.dot(x * x, jnp.ones((HD, HD), BF16), preferred_element_type=F32)
    return jnp.max(sums.reshape(-1, 8, HD), axis=0)


def span_of(doc_blocks, doc):
    def find(d, carry):
        total, start, end = carry
        size = doc_blocks[d]
        start = jnp.where(d == doc, total, start)
        end = jnp.where(d == doc, total + size, end)
        return (total + size, start, end)

    zero = jnp.int32(0)
    _, start, end = lax.fori_loop(0, doc_blocks.shape[0], find, (zero, zero, zero), unroll=True)
    return start * BLK, end * BLK


def causal_mask(n):
    return lax.broadcasted_iota(jnp.int32, (n, n), 1) <= lax.broadcasted_iota(jnp.int32, (n, n), 0)


def whole_number(ref, place):
    return jnp.max(ref[16 * place : 16 * place + 16].astype(F32)).astype(jnp.int32)


def turning(table, offset_hi, offset_lo, rows):
    ca, sa = table[pl.ds(offset_hi, 1), :], table[pl.ds(offset_hi + COARSE, 1), :]
    cb = table[pl.ds(offset_lo + 2 * COARSE, 1), :]
    sb = table[pl.ds(offset_lo + 2 * COARSE + rows, 1), :]
    c1 = ca * cb - sa * sb
    s1 = sa * cb + ca * sb
    c2 = table[2 * COARSE : 2 * COARSE + rows, :]
    s2 = table[2 * COARSE + rows : 2 * COARSE + 2 * rows, :]
    return c1 * c2 - s1 * s2, s1 * c2 + c1 * s2


def stage_kernel(chunks, all_chunks, slots, count, first, last, head, *refs):
    refs = list(refs)
    take = lambda n: [refs.pop(0) for _ in range(n)]
    (ids,) = take(1)
    if first:
        doc_blocks, own_doc, own_offset, table, *own_reader, side = take(8)
    else:
        spans, q_ref, k_ref, v_ref = take(4)
    pieces = take(len(slots))
    if not first:
        acc_in, bound_in = take(2)
    if last:
        if head:
            take(1)
        own_out, side_out, acc_ref, bound_ref, out, peak_ref, total_ref = take(7)
    elif first:
        acc_ref, bound_ref, spans, q_ref, k_ref, v_ref = take(6)
    else:
        acc_ref, bound_ref = take(2)
    kbuf, vbuf = take(2)
    kvh = head if last else pl.program_id(0)
    reader = pl.program_id(0 if last else 1)
    me = ids[2]
    acc = acc_ref.at[reader, kvh]
    most = bound_ref.at[reader, kvh, 0:8]
    q_rows = q_ref.at[reader, kvh]
    k_own, v_own = k_ref.at[reader, kvh], v_ref.at[reader, kvh]
    rows = k_own.shape[0]

    def part(p, col):
        place = pl.ds(pl.multiple_of((col + kvh) * HD, HD), HD)
        return pieces[p][slots[p] * count : (slots[p] + 1) * count, place]

    heads = q_rows.shape[0] // rows
    tile = ROW_TILE_HEADS * rows
    tiles = heads // ROW_TILE_HEADS
    at = lambda t: slice(t * tile, (t + 1) * tile)

    if first:
        lead = 2 * heads

        def side_part(col):
            return side[:, pl.ds(pl.multiple_of(col * HD, HD), HD)]

        for r in range(2):

            @pl.when(reader == r)
            def _(r=r):
                if r == 0:
                    document = own_doc[0]
                    offset = jnp.clip(own_offset[0], 0, COARSE * COARSE - 1)
                    hi = offset // COARSE
                    lo = offset - hi * COARSE
                    raw_q = lambda h: own_reader[0][:, h * HD : (h + 1) * HD]
                    raw_k, raw_v = own_reader[1][...], own_reader[2][...]
                else:
                    numbers = side_part(lead + 2 * HALF_KV)
                    document, hi, lo = [whole_number(numbers, i) for i in range(3)]
                    raw_q = lambda h: side_part(kvh * heads + h)
                    raw_k, raw_v = side_part(lead + kvh), side_part(lead + HALF_KV + kvh)
                begin, finish = span_of(doc_blocks, document)
                spans[2 * r] = begin
                spans[2 * r + 1] = finish
                cosine, sine = turning(table, hi, lo, rows)

                def rotated(x):
                    x = x.astype(F32)
                    return (x * cosine + pltpu.roll(x, HD // 2, 1) * sine).astype(BF16)

                k_own[...] = rotated(raw_k)
                v_own[...] = raw_v
                for h in range(heads):
                    q_rows[h * rows : (h + 1) * rows, :] = rotated(raw_q(h))

    start = spans[2 * reader]
    end = spans[2 * reader + 1]

    if first:
        mask = jnp.concatenate([causal_mask(rows)] * ROW_TILE_HEADS, axis=0)
        keys = k_own[...]
        values = jnp.concatenate([v_own[...], jnp.ones((rows, HD), BF16)], axis=1)
        q_most = jnp.zeros((8, HD), F32)
        for t in range(tiles):
            q = q_rows[at(t), :]
            weights = jnp.exp2(scores_of(q, keys) * EXP2_SCALE)
            weights = jnp.where(mask, weights, 0.0).astype(BF16)
            acc[at(t), :] = jnp.dot(weights, values, preferred_element_type=F32)
            q_most = jnp.maximum(q_most, square_bound(q))
        most[...] = square_bound(keys)
        bound_ref[reader, kvh, 8:16, :] = q_most

    if not chunks:
        return
    filled = jnp.int32(0)
    for p in range(0, len(chunks), 2):
        bases = [chunks[p + i](me) * count for i in range(2)]
        lows = [jnp.maximum(base, start) for base in bases]
        shown = [
            jnp.maximum(jnp.minimum(base + count, end) - low, 0)
            for base, low in zip(bases, lows, strict=True)
        ]
        ahead = [jnp.where(bases[i] > bases[1 - i], shown[1 - i], 0) for i in range(2)]
        for i in range(2):

            @pl.when(shown[i] > 0)
            def _(p=p + i, put=count + filled + ahead[i] + bases[i] - lows[i]):
                to = pl.ds(pl.multiple_of(put, BLK), count)
                kbuf[to, :] = part(p, 0)
                vbuf[to, 0:HD] = part(p, HALF_KV)
                vbuf[to, HD:] = jnp.ones((count, HD), BF16)

        filled = filled + shown[0] + shown[1]
    some = filled > 0

    @pl.when(some)
    def _():
        to = pl.ds(pl.multiple_of(count + filled, BLK), count)
        kbuf[to, :] = jnp.zeros((count, HD), BF16)
        vbuf[to, :] = jnp.zeros((count, 2 * HD), BF16)

    def attend(step, _):
        here = pl.ds(pl.multiple_of(count + step * count, BLK), count)
        keys = kbuf[here, :]
        values = vbuf[here, :]
        most[...] = jnp.maximum(most[...], square_bound(keys))
        for t in range(tiles):
            weights = jnp.exp2(scores_of(q_rows[at(t), :], keys) * EXP2_SCALE).astype(BF16)
            acc[at(t), :] += jnp.dot(weights, values, preferred_element_type=F32)
        return 0

    lax.fori_loop(0, (filled + count - 1) // count, attend, 0)
    if last:
        q_most = jnp.max(bound_ref[reader, kvh, 8:16, :])
        safe = jnp.max(most[...]) * q_most <= (SAFE_LOG2 / EXP2_SCALE) ** 2

        @pl.when(safe)
        def _():
            for h in range(heads):
                mine = slice(h * rows, (h + 1) * rows)
                out[:, h * HD : (h + 1) * HD] = (acc[mine, :HD] / acc[mine, HD:]).astype(BF16)

        @pl.when(jnp.logical_not(safe))
        def _():
            def absorb(h, keys, values, shown, fresh):
                mine = pl.ds(pl.multiple_of(h * rows, rows), rows)
                s = jnp.where(shown, scores_of(q_rows[mine, :], keys) * score_scale, masked_score)
                most_now = jnp.max(s, axis=1, keepdims=True)
                if fresh:
                    peak = jnp.broadcast_to(most_now, (rows, HD))
                else:
                    before = peak_ref[mine, :]
                    peak = jnp.maximum(before, most_now)
                w = jnp.where(shown, jnp.exp(s - peak[:, :1]), 0.0)
                total = jnp.broadcast_to(jnp.sum(w, axis=1, keepdims=True), (rows, HD))
                gained = jnp.dot(w.astype(BF16), values, preferred_element_type=F32)
                if not fresh:
                    factor = jnp.exp(before - peak)
                    total = total + total_ref[mine, :] * factor
                    gained = gained + acc[mine, 0:HD] * factor
                peak_ref[mine, :] = peak
                total_ref[mine, :] = total
                acc[mine, 0:HD] = gained

            def own(h, _):
                absorb(h, k_own[...], v_own[...], causal_mask(rows), True)
                return 0

            lax.fori_loop(0, heads, own, 0)
            for p, chunk in enumerate(all_chunks):
                base = chunk(me) * count

                @pl.when((base < end) & (base + count > start))
                def _(p=p, base=base):
                    token = base + lax.broadcasted_iota(jnp.int32, (rows, count), 1)
                    shown = (token >= start) & (token < end)

                    def body(h, _):
                        absorb(h, part(p, 0), part(p, HALF_KV), shown, False)
                        return 0

                    lax.fori_loop(0, heads, body, 0)

            def finish(h, _):
                mine = pl.ds(pl.multiple_of(h * rows, rows), rows)
                out[:, pl.ds(pl.multiple_of(h * HD, HD), HD)] = (
                    acc[mine, 0:HD] / total_ref[mine, :]
                ).astype(BF16)
                return 0

            lax.fori_loop(0, heads, finish, 0)

        for r, done in enumerate((own_out, side_out)):

            @pl.when(reader == r)
            def _(done=done):
                done[...] = out[...]


def stage(ids, inputs, pieces_now, state, kept, everything=None, head=0, whole=None, name="stage"):
    first = state is None
    last = everything is not None
    smem = pl.BlockSpec(memory_space=pltpu.SMEM)
    count = kept["count"]
    rows, heads = kept["rows"], kept["heads"]
    here = pl.BlockSpec(memory_space=pltpu.VMEM)
    pieces = everything or pieces_now
    args = [ids]
    specs = []
    for a, spec in inputs:
        args.append(a)
        specs.append(smem if spec == "scalar" else here if spec == "whole" else spec)
    if not first:
        args += [kept["spans"], kept["q"], kept["k"], kept["v"]]
        specs += [smem, here, here, here]
    args += [a for a, _, _ in pieces]
    specs += [here] * len(pieces)
    aliases = {}
    full = lambda *shape: (2, HALF_KV) + shape
    out_shape = [
        jax.ShapeDtypeStruct(full(heads * rows, 2 * HD), F32),
        jax.ShapeDtypeStruct(full(16, HD), F32),
    ]
    out_specs = [here, here]
    scratch = []
    if first:
        out_shape += [
            jax.ShapeDtypeStruct((4,), jnp.int32),
            jax.ShapeDtypeStruct(full(heads * rows, HD), BF16),
            jax.ShapeDtypeStruct(full(rows, HD), BF16),
            jax.ShapeDtypeStruct(full(rows, HD), BF16),
        ]
        out_specs += [smem, here, here, here]
    else:
        aliases = {len(args) + i: (2 if last else 0) + i for i in range(2)}
        args += list(state)
        specs += [here, here]
    if last:
        group = heads * HD
        out_shape = [
            jax.ShapeDtypeStruct((rows, 2 * HALF_KV * group), BF16),
            jax.ShapeDtypeStruct((rows, group), BF16),
        ] + out_shape
        out_specs = [
            pl.BlockSpec((rows, group), lambda r, ids: (0, ids[0] * HALF_KV + head)),
            here,
        ] + out_specs
        if head:
            aliases[len(args)] = 0
            args.append(whole)
            specs.append(pl.BlockSpec(memory_space=pl.ANY))
        scratch = [
            pltpu.VMEM((rows, group), BF16),
            pltpu.VMEM((heads * rows, HD), F32),
            pltpu.VMEM((heads * rows, HD), F32),
        ]
    scratch += [
        pltpu.VMEM(((len(pieces_now) + 2) * count, HD), BF16),
        pltpu.VMEM(((len(pieces_now) + 2) * count, 2 * HD), BF16),
    ]
    return pl.pallas_call(
        functools.partial(
            stage_kernel,
            [chunk for _, _, chunk in pieces_now],
            [chunk for _, _, chunk in everything or ()],
            [part for _, part, _ in pieces],
            count,
            first,
            last,
            head,
        ),
        grid_spec=pltpu.PrefetchScalarGridSpec(
            num_scalar_prefetch=1,
            grid=(2,) if last else (HALF_KV, 2),
            in_specs=specs,
            out_specs=out_specs,
            scratch_shapes=scratch,
        ),
        out_shape=out_shape,
        input_output_aliases=aliases,
        compiler_params=pltpu.CompilerParams(vmem_limit_bytes=VMEM),
        cost_estimate=pl.CostEstimate(
            flops=15000000000 if first else 10000000000,
            bytes_accessed=1 << 18,
            transcendentals=0,
        ),
        name=name,
    )(*args)


def shards(
    prompt_queries,
    prompt_keys,
    prompt_values,
    cache_keys,
    cache_values,
    doc_blocks,
    reader_docs,
    reader_offsets,
):
    size = lax.axis_size("docs")
    me = lax.axis_index("docs").astype(jnp.int32)
    tokens = cache_keys.shape[0]
    half = lax.rem(me, 2)

    def moved(x, pairs):
        return lax.ppermute(
            x, "docs", [(i, j) for i, j in pairs if 0 <= i < size and 0 <= j < size]
        )

    everyone = range(size)
    second = lambda i: (i // 2) % 2
    beside = lambda x: moved(x, [(i, i ^ 1) for i in everyone])
    across = lambda x: moved(x, [(i, i ^ 2) for i in everyone])
    across_other = lambda x: moved(x, [(i, i ^ 3) for i in everyone])
    onward = lambda x: moved(x, [(i, i + 4) for i in everyone])
    onward_other = lambda x: moved(x, [(i, (i + 4) ^ 1) for i in everyone])
    back = lambda x: moved(x, [(i, i - 4) for i in everyone])
    back_other = lambda x: moved(x, [(i, (i - 4) ^ 1) for i in everyone])
    next_other = lambda x: moved(
        x, [(i, (i + 2) ^ 1 if second(i) else (i - 2) ^ 1) for i in everyone]
    )
    relay = lambda x: moved(x, [(i, i - 4 if second(i) else i + 4) for i in everyone])

    rows = prompt_queries.shape[0]
    block_rows = angle_rows(np.arange(COARSE) * BLK, attention_gain)
    coarse_rows = angle_rows(np.arange(COARSE) * COARSE, attention_gain)
    cache_table = np.concatenate(block_rows + angle_rows(np.arange(BLK), 1.0))
    query_table = np.concatenate(coarse_rows + angle_rows(np.arange(rows), 1.0))

    ids = jnp.stack([half, me * (tokens // BLK), me])
    columns = prompt_queries.shape[1] // 2
    width = prompt_keys.shape[1] // 2
    mine, theirs, message = prepare_cache(
        doc_blocks,
        reader_docs,
        reader_offsets,
        jnp.asarray(cache_table),
        cache_keys,
        cache_values,
        (prompt_queries, prompt_keys, prompt_values),
    )
    side = beside(message)
    other = beside(theirs)
    across_a = across(mine)
    chip = jnp.concatenate([mine, other], axis=0)
    onward_c = onward(chip)
    back_c = back(chip)
    across_b = across_other(lax.optimization_barrier((theirs, chip))[0])

    near = [(mine, 0, lambda i: i), (other, 0, lambda i: i ^ 1)]
    group = columns // HALF_KV
    mine_at = lambda k, r, ids: (0, ids[0] * HALF_KV + k)
    wide = lambda place: pl.BlockSpec((rows, group), place)
    thin = lambda place: pl.BlockSpec((rows, HD), place)
    table = jnp.asarray(query_table)
    inputs = [
        (doc_blocks, "scalar"),
        (reader_docs, "scalar"),
        (reader_offsets, "scalar"),
        (table, "whole"),
        (prompt_queries, wide(mine_at)),
        (prompt_keys, thin(mine_at)),
        (prompt_values, thin(mine_at)),
        (side, "whole"),
    ]
    kept = {"count": tokens, "rows": rows, "heads": group // HD}
    acc, bound, spans, turned_q, turned_k, kept_v = stage(
        ids, inputs, [], None, kept, name="alone"
    )
    bound, theirs, passing = lax.optimization_barrier((bound, theirs, across_a))
    far_a = relay(passing)
    far_b = next_other(theirs)
    kept.update(spans=spans, q=turned_q, k=turned_k, v=kept_v)
    middle = [
        (onward_c, 0, lambda i: i - 4),
        (onward_c, 1, lambda i: (i - 4) ^ 1),
        (across_a, 0, lambda i: i ^ 2),
        (across_b, 0, lambda i: i ^ 3),
        (back_c, 0, lambda i: i + 4),
        (back_c, 1, lambda i: (i + 4) ^ 1),
    ]
    state = stage(ids, [], near, (acc, bound), kept, name="near")
    state = stage(ids, [], middle, state, kept, name="middle")

    partner = lambda i: i - 2 + 4 * ((i >> 1) & 1)
    far = [(far_a, 0, partner), (far_b, 0, lambda i: partner(i) ^ 1)]
    everything = far + near + middle
    whole, sides = None, []
    for head in range(HALF_KV):
        whole, side_out, *state = stage(
            ids, [], far, state, kept, everything, head, whole, name="far"
        )
        sides.append(beside(side_out))
    for head, came in enumerate(sides):
        column = (1 - half) * columns + head * group
        whole = lax.dynamic_update_slice(whole, came, (jnp.int32(0), column))
    return whole


def solution(mesh):
    both = P(("groups", "docs"))
    wide = P(("groups", "docs"), None)
    placed = (wide, wide, wide, wide, wide, P("groups"), both, both)
    return jax.shard_map(shards, mesh=mesh, in_specs=placed, out_specs=wide, check_vma=False)
```

profile of v0, /device:TPU:21, one launch (start us, length us, event | category | flops | bytes accessed | tf_op | source)
XLA Modules:
  0.0 257.0 jit_solution(7162422044203789626)
XLA Ops:
  1.3 0.0 copy-start
  1.3 0.0 copy-start.2
  1.3 0.0 copy-start.3
  1.3 0.0 copy-start.4
  1.3 4.3 %prepare_cache.1 = (bf16[512,512]{1,0:T(8,128)(2,1)}, bf16[512,512]{1,0:T(8,128)(2,1)}, bf16[128,4736]{1,0:T(8,128)(2,1)}) custom-call(s32[8]{0:T(128)} %refs_1_.1, s32[1]{0:T(128)S(6)} %copy.32.doc.refs_2_, s32[1]{0:T(128)S(6)} %copy.33.offset.refs_3_, f32[192,128]{1,0:T(8,128)} %constant.25.clone.table, bf16[512,512]{1,0:T(8,128)(2,1)} %k_ref.1, ...), custom_call_target="tpu_custom_call" | custom-call | flops 4000000 | bytes 4194304 | tf_op jit(solution)/shard_map/prepare_cache/pallas_call | solution.py:136
  5.6 0.7 collective-permute-start
  6.3 0.1 collective-permute-start.4
  6.4 0.2 collective-permute-start.1
  6.6 0.0 copy-start.6
  6.6 0.0 copy-start.5
  6.6 0.1 pad_add_fusion.refs_0_
  6.7 1.1 constant_dynamic-update-slice_fusion.1
  7.8 1.8 collective-permute-done.4.refs_6_.refs_8_
  9.7 0.0 copy-start.1
  9.7 3.3 %collective-permute-start.5 = (bf16[1024,512]{1,0:T(8,128)(2,1)S(1)}, bf16[1024,512]{1,0:T(8,128)(2,1)S(1)}, u32[]{:S(2)}, u32[]{:S(2)}) collective-permute-start(bf16[1024,512]{1,0:T(8,128)(2,1)S(1)} %constant_dynamic-update-slice_fusion), channel_id=1, source_target_pairs={{0,4},{1,5},{2,6},{3,7},{4,8},{5,9},{6,10},{7,11},{8,12},{9,13},{1... | collective-permute-start | bytes 3145736 | tf_op jit(solution)/shard_map/ppermute | solution.py:497
  13.1 2.1 collective-permute-start.7
  15.1 0.0 copy-done.6
  15.2 1.0 collective-permute-start.6
  16.1 0.0 collective-permute-done.refs_8_
  16.1 0.0 copy-done
  16.1 0.0 copy-done.2
  16.1 0.0 copy-done.3
  16.1 0.0 copy-done.4
  16.2 0.0 copy-done.5
  16.2 7.6 %alone.1 = (f32[2,2,2048,256]{3,2,1,0:T(8,128)S(1)}, f32[2,2,16,128]{3,2,1,0:T(8,128)S(1)}, s32[4]{0:T(128)S(1)}, bf16[2,2,2048,128]{3,2,1,0:T(8,128)(2,1)S(1)},...) custom-call(s32[3]{0:T(128)S(1)} %pad_add_fusion.refs_0_, s32[8]{0:T(128)S(1)} %copy-done.4, ...), custom_call_target="tpu_custom_call" | custom-call | flops 15000000512 | bytes 262144 | tf_op jit(solution)/shard_map/alone/pallas_call | solution.py:451
  23.8 0.0 collective-permute-done.1.refs_7_.refs_11_
  23.8 2.1 collective-permute-start.2
  26.0 3.0 %collective-permute-start.3 = (bf16[512,512]{1,0:T(8,128)(2,1)S(1)}, bf16[512,512]{1,0:T(8,128)(2,1)S(1)}, u32[]{:S(2)}, u32[]{:S(2)}) collective-permute-start(bf16[512,512]{1,0:T(8,128)(2,1)S(1)} %copy-done.6), channel_id=1, source_target_pairs={{2,5},{3,4},{4,3},{5,2},{6,9},{7,8},{8,7},{9,6},{10,13},{11,12},{1... | collective-permute-start | bytes 1572872 | tf_op jit(solution)/shard_map/ppermute | solution.py:497
  29.0 0.0 copy-done.1
  29.0 12.3 %near.1 = (f32[2,2,2048,256]{3,2,1,0:T(8,128)S(1)}, f32[2,2,16,128]{3,2,1,0:T(8,128)S(1)}) custom-call(s32[3]{0:T(128)S(1)} %pad_add_fusion.refs_0_, s32[4]{0:T(128)S(1)} %get-tuple-element.29.refs_1_, bf16[2,2,2048,128]{3,2,1,0:T(8,128)(2,1)S(1)} %get-tuple-element.30.refs_2_, ...), custom_call_target="tpu_custom_call", output_to_operand_aliasing={{0}: (7, {}), {1}: (8, {})} | custom-call | flops 10000000000 | bytes 262144 | tf_op jit(solution)/shard_map/near/pallas_call | solution.py:451
  41.2 0.0 collective-permute-done.6.refs_8_.refs_12_
  41.3 0.0 collective-permute-done.5.refs_5_.refs_6_.refs_9_.refs_10_
  41.3 0.0 collective-permute-done.7.refs_9_.refs_10_.refs_13_.refs_14_
  41.3 12.4 %middle.1 = (f32[2,2,2048,256]{3,2,1,0:T(8,128)S(1)}, f32[2,2,16,128]{3,2,1,0:T(8,128)S(1)}) custom-call(s32[3]{0:T(128)S(1)} %pad_add_fusion.refs_0_, s32[4]{0:T(128)S(1)} %get-tuple-element.29.refs_1_, bf16[2,2,2048,128]{3,2,1,0:T(8,128)(2,1)S(1)} %get-tuple-element.30.refs_2_, ...), custom_call_target="tpu_custom_call", output_to_operand_aliasing={{0}: (11, {}), {1}: (12, {})} | custom-call | flops 10000000000 | bytes 262144 | tf_op jit(solution)/shard_map/middle/pallas_call | solution.py:451
  53.7 0.0 collective-permute-done.2.refs_5_
  53.7 0.0 collective-permute-done.3.refs_6_
  53.8 99.9 %far.2 = (bf16[128,8192]{1,0:T(8,128)(2,1)}, bf16[128,2048]{1,0:T(8,128)(2,1)S(1)}, f32[2,2,2048,256]{3,2,1,0:T(8,128)S(1)}, f32[2,2,16,128]{3,2,1,0:T(8,128)S(1)}) custom-call(s32[3]{0:T(128)S(1)} %pad_add_fusion.refs_0_, s32[4]{0:T(128)S(1)} %get-tuple-element.29.refs_1_, ...), custom_call_target="tpu_custom_call", output_to_operand_aliasing={{2}: (15, {}), {3}: (16, {})} | custom-call | flops 10000000000 | bytes 262144 | tf_op jit(solution)/shard_map/far/pallas_call | solution.py:451
  153.7 0.5 collective-permute-start.8
  154.2 100.0 %far.3 = (bf16[128,8192]{1,0:T(8,128)(2,1)}, bf16[128,2048]{1,0:T(8,128)(2,1)S(1)}, f32[2,2,2048,256]{3,2,1,0:T(8,128)S(1)}, f32[2,2,16,128]{3,2,1,0:T(8,128)S(1)}) custom-call(s32[3]{0:T(128)S(1)} %pad_add_fusion.refs_0_, s32[4]{0:T(128)S(1)} %get-tuple-element.29.refs_1_, ...), custom_call_target="tpu_custom_call", output_to_operand_aliasing={{2}: (15, {}), {3}: (16, {}), {0}: (17, {})} | custom-call | flops 10000000000 | bytes 262144 | tf_op jit(solution)/shard_map/far/pallas_call | solution.py:451
  254.2 0.0 collective-permute-start.9
  254.2 0.0 collective-permute-done.8
  254.2 0.8 constant_dynamic-update-slice_fusion.3
  255.0 1.1 collective-permute-done.9
  256.1 0.8 constant_dynamic-update-slice_fusion.2
  (1 shorter events, 0.0 us)
Async XLA Ops:
  1.3 14.8 %copy-start = (bf16[128,8192]{1,0:T(8,128)(2,1)S(1)}, bf16[128,8192]{1,0:T(8,128)(2,1)}, u32[]{:S(2)}) copy-start(bf16[128,8192]{1,0:T(8,128)(2,1)} %refs_5_.1) | copy-start | bytes 6291460
  1.3 14.8 %copy-start.2 = (bf16[128,512]{1,0:T(8,128)(2,1)S(1)}, bf16[128,512]{1,0:T(8,128)(2,1)}, u32[]{:S(2)}) copy-start(bf16[128,512]{1,0:T(8,128)(2,1)} %refs_6_.1) | copy-start | bytes 393220
  1.3 14.8 %copy-start.3 = (bf16[128,512]{1,0:T(8,128)(2,1)S(1)}, bf16[128,512]{1,0:T(8,128)(2,1)}, u32[]{:S(2)}) copy-start(bf16[128,512]{1,0:T(8,128)(2,1)} %refs_7_.1) | copy-start | bytes 393220
  1.3 14.8 %copy-start.4 = (s32[8]{0:T(128)S(1)}, s32[8]{0:T(128)}, u32[]{:S(2)}) copy-start(s32[8]{0:T(128)} %refs_1_.1) | copy-start | bytes 100
  5.6 10.5 %collective-permute-start = (bf16[128,4736]{1,0:T(8,128)(2,1)}, bf16[128,4736]{1,0:T(8,128)(2,1)}, u32[]{:S(2)}, u32[]{:S(2)}) collective-permute-start(bf16[128,4736]{1,0:T(8,128)(2,1)} %get-tuple-element.28), channel_id=1, source_target_pairs={{0,1},{1,0},{2,3},{3,2},{4,5},{5,4},{6,7},{7,6},{8,9},{9,8},{10,11... | collective-permute-start | bytes 3637256 | tf_op jit(solution)/shard_map/ppermute | solution.py:497
  6.3 3.3 %collective-permute-start.4 = (bf16[512,512]{1,0:T(8,128)(2,1)}, bf16[512,512]{1,0:T(8,128)(2,1)S(1)}, u32[]{:S(2)}, u32[]{:S(2)}) collective-permute-start(bf16[512,512]{1,0:T(8,128)(2,1)} %get-tuple-element.38), channel_id=1, source_target_pairs={{0,1},{1,0},{2,3},{3,2},{4,5},{5,4},{6,7},{7,6},{8,9},{9,8},{10,11... | collective-permute-start | bytes 1572872 | tf_op jit(solution)/shard_map/ppermute | solution.py:497
  6.4 17.4 %collective-permute-start.1 = (bf16[512,512]{1,0:T(8,128)(2,1)}, bf16[512,512]{1,0:T(8,128)(2,1)S(1)}, u32[]{:S(2)}, u32[]{:S(2)}) collective-permute-start(bf16[512,512]{1,0:T(8,128)(2,1)} %get-tuple-element.35.refs_5_.refs_7_), channel_id=1, source_target_pairs={{0,2},{1,3},{2,0},{3,1},{4,6},{5,7},{6,4},{7,5},{8,10},{9,11},{10,... | collective-permute-start | bytes 1572872 | tf_op jit(solution)/shard_map/ppermute | solution.py:497
  6.6 8.5 %copy-start.6 = (bf16[512,512]{1,0:T(8,128)(2,1)S(1)}, bf16[512,512]{1,0:T(8,128)(2,1)}, u32[]{:S(2)}) copy-start(bf16[512,512]{1,0:T(8,128)(2,1)} %get-tuple-element.38) | copy-start | bytes 1572868
  6.6 9.5 %copy-start.5 = (f32[384,128]{1,0:T(8,128)S(1)}, f32[384,128]{1,0:T(8,128)}, u32[]{:S(2)}) copy-start(f32[384,128]{1,0:T(8,128)} %constant.26.clone.refs_4_) | copy-start | bytes 589828
  9.7 19.3 %copy-start.1 = (bf16[512,512]{1,0:T(8,128)(2,1)S(1)}, bf16[512,512]{1,0:T(8,128)(2,1)}, u32[]{:S(2)}) copy-start(bf16[512,512]{1,0:T(8,128)(2,1)} %get-tuple-element.35.refs_5_.refs_7_) | copy-start | bytes 1572868
  9.7 31.5 %collective-permute-start.5 = (bf16[1024,512]{1,0:T(8,128)(2,1)S(1)}, bf16[1024,512]{1,0:T(8,128)(2,1)S(1)}, u32[]{:S(2)}, u32[]{:S(2)}) collective-permute-start(bf16[1024,512]{1,0:T(8,128)(2,1)S(1)} %constant_dynamic-update-slice_fusion), channel_id=1, source_target_pairs={{0,4},{1,5},{2,6},{3,7},{4,8},{5,9},{6,10},{7,11},{8,12},{9,13},{1... | collective-permute-start | bytes 3145736 | tf_op jit(solution)/shard_map/ppermute | solution.py:497
  13.1 28.2 %collective-permute-start.7 = (bf16[1024,512]{1,0:T(8,128)(2,1)S(1)}, bf16[1024,512]{1,0:T(8,128)(2,1)S(1)}, u32[]{:S(2)}, u32[]{:S(2)}) collective-permute-start(bf16[1024,512]{1,0:T(8,128)(2,1)S(1)} %constant_dynamic-update-slice_fusion), channel_id=1, source_target_pairs={{4,0},{5,1},{6,2},{7,3},{8,4},{9,5},{10,6},{11,7},{12,8},{13,9},{1... | collective-permute-start | bytes 3145736 | tf_op jit(solution)/shard_map/ppermute | solution.py:497
  15.2 26.1 %collective-permute-start.6 = (bf16[512,512]{1,0:T(8,128)(2,1)S(1)}, bf16[512,512]{1,0:T(8,128)(2,1)S(1)}, u32[]{:S(2)}, u32[]{:S(2)}) collective-permute-start(bf16[512,512]{1,0:T(8,128)(2,1)S(1)} %copy-done.6), channel_id=1, source_target_pairs={{0,3},{1,2},{2,1},{3,0},{4,7},{5,6},{6,5},{7,4},{8,11},{9,10},{10,... | collective-permute-start | bytes 1572872 | tf_op jit(solution)/shard_map/ppermute | solution.py:497
  23.8 29.9 %collective-permute-start.2 = (bf16[512,512]{1,0:T(8,128)(2,1)S(1)}, bf16[512,512]{1,0:T(8,128)(2,1)S(1)}, u32[]{:S(2)}, u32[]{:S(2)}) collective-permute-start(bf16[512,512]{1,0:T(8,128)(2,1)S(1)} %collective-permute-done.1.refs_7_.refs_11_), channel_id=1, source_target_pairs={{0,4},{1,5},{4,8},{5,9},{6,2},{7,3},{8,12},{9,13},{10,6},{11,7},{1... | collective-permute-start | bytes 1572872 | tf_op jit(solution)/shard_map/ppermute | solution.py:497
  26.0 27.8 %collective-permute-start.3 = (bf16[512,512]{1,0:T(8,128)(2,1)S(1)}, bf16[512,512]{1,0:T(8,128)(2,1)S(1)}, u32[]{:S(2)}, u32[]{:S(2)}) collective-permute-start(bf16[512,512]{1,0:T(8,128)(2,1)S(1)} %copy-done.6), channel_id=1, source_target_pairs={{2,5},{3,4},{4,3},{5,2},{6,9},{7,8},{8,7},{9,6},{10,13},{11,12},{1... | collective-permute-start | bytes 1572872 | tf_op jit(solution)/shard_map/ppermute | solution.py:497
  153.7 100.6 %collective-permute-start.8 = (bf16[128,2048]{1,0:T(8,128)(2,1)S(1)}, bf16[128,2048]{1,0:T(8,128)(2,1)S(1)}, u32[]{:S(2)}, u32[]{:S(2)}) collective-permute-start(bf16[128,2048]{1,0:T(8,128)(2,1)S(1)} %get-tuple-element.49), channel_id=1, source_target_pairs={{0,1},{1,0},{2,3},{3,2},{4,5},{5,4},{6,7},{7,6},{8,9},{9,8},{10,11... | collective-permute-start | bytes 1572872 | tf_op jit(solution)/shard_map/ppermute | solution.py:497
  254.2 1.9 collective-permute-start.9
where the time goes:
time: 259 us; the launch traced here: 257 us
  Pallas kernels  237 us (92%)
  starting transfers between devices  13 us (5%)
  waiting for transfers between devices  2.93 us (1%)
  local copies, waits for them, and re-layouts  2.86 us (1%)
    pallas_call x5, Pallas kernels, stage(): pl.pallas_call(functools.partial(stage_kernel, [chunk for _, _, chunk in...  232 us
    ppermute x10, starting transfers between devices, moved(): lax.ppermute(x, 'docs', [(i, j) for i, j in pairs if 0 <= i < size and 0...  13 us
  transfers between devices with their start and end apart: 10, of which 2 were waited for; matrix products, arithmetic and copies ran while one was open for 1% of the time, Pallas kernels for 52%

commit v1 on v0

--- a/solution.py
+++ b/solution.py
@@ -309,8 +309,8 @@
         kbuf[to, :] = jnp.zeros((count, HD), BF16)
         vbuf[to, :] = jnp.zeros((count, 2 * HD), BF16)
 
-    def attend(step, _):
-        here = pl.ds(pl.multiple_of(count + step * count, BLK), count)
+    def attend(step, _, size=count):
+        here = pl.ds(pl.multiple_of(count + step * count, BLK), size)
         keys = kbuf[here, :]
         values = vbuf[here, :]
         most[...] = jnp.maximum(most[...], square_bound(keys))
@@ -319,7 +319,14 @@
             acc[at(t), :] += jnp.dot(weights, values, preferred_element_type=F32)
         return 0
 
-    lax.fori_loop(0, (filled + count - 1) // count, attend, 0)
+    half = count // 2
+    steps = (filled + half - 1) // count
+    lax.fori_loop(0, steps, attend, 0)
+
+    @pl.when(filled > steps * count)
+    def _():
+        attend(steps, 0, half)
+
     if last:
         q_most = jnp.max(bound_ref[reader, kvh, 8:16, :])
         safe = jnp.max(most[...]) * q_most <= (SAFE_LOG2 / EXP2_SCALE) ** 2

time: 259 us -> 257 us (level)
  the two profiles are of different devices: /device:TPU:21 before, /device:TPU:17 now
where the time goes in v1:
time: 257 us; the launch traced here: 256 us
  Pallas kernels  234 us (91%)
  starting transfers between devices  15.6 us (6%)
  local copies, waits for them, and re-layouts  2.86 us (1%)
    pallas_call x5, Pallas kernels, stage(): pl.pallas_call(functools.partial(stage_kernel, [chunk for _, _, chunk in...  230 us
    ppermute x10, starting transfers between devices, moved(): lax.ppermute(x, 'docs', [(i, j) for i, j in pairs if 0 <= i < size and 0...  15.6 us
  transfers between devices with their start and end apart: 10, of which 2 were waited for; matrix products, arithmetic and copies ran while one was open for 1% of the time, Pallas kernels for 51%

profile of v1, /device:TPU:17, one launch (start us, length us, event | category | flops | bytes accessed | tf_op | source)
XLA Modules:
  0.0 255.9 jit_solution(9855213766793397668)
XLA Ops:
  1.3 0.0 copy-start
  1.3 0.0 copy-start.2
  1.3 0.0 copy-start.3
  1.3 0.0 copy-start.4
  1.3 4.3 %prepare_cache.1 = (bf16[512,512]{1,0:T(8,128)(2,1)}, bf16[512,512]{1,0:T(8,128)(2,1)}, bf16[128,4736]{1,0:T(8,128)(2,1)}) custom-call(s32[8]{0:T(128)} %refs_1_.1, s32[1]{0:T(128)S(6)} %copy.32.doc.refs_2_, s32[1]{0:T(128)S(6)} %copy.33.offset.refs_3_, f32[192,128]{1,0:T(8,128)} %constant.25.clone.table, bf16[512,512]{1,0:T(8,128)(2,1)} %k_ref.1, ...), custom_call_target="tpu_custom_call" | custom-call | flops 4000000 | bytes 4194304 | tf_op jit(solution)/shard_map/prepare_cache/pallas_call | solution.py:136
  5.6 0.7 collective-permute-start
  6.3 0.1 collective-permute-start.4
  6.4 1.2 collective-permute-start.1
  7.6 0.0 copy-start.6
  7.6 0.0 copy-start.5
  7.6 0.1 pad_add_fusion.refs_0_
  7.7 1.1 constant_dynamic-update-slice_fusion.1
  8.8 0.8 collective-permute-done.4.refs_6_.refs_8_
  9.7 0.0 copy-start.1
  9.7 3.3 %collective-permute-start.5 = (bf16[1024,512]{1,0:T(8,128)(2,1)S(1)}, bf16[1024,512]{1,0:T(8,128)(2,1)S(1)}, u32[]{:S(2)}, u32[]{:S(2)}) collective-permute-start(bf16[1024,512]{1,0:T(8,128)(2,1)S(1)} %constant_dynamic-update-slice_fusion), channel_id=1, source_target_pairs={{0,4},{1,5},{2,6},{3,7},{4,8},{5,9},{6,10},{7,11},{8,12},{9,13},{1... | collective-permute-start | bytes 3145736 | tf_op jit(solution)/shard_map/ppermute | solution.py:504
  13.1 2.1 collective-permute-start.7
  15.1 0.0 copy-done.6
  15.2 2.0 collective-permute-start.6
  17.1 0.0 collective-permute-done.refs_8_
  17.1 0.0 copy-done
  17.1 0.0 copy-done.2
  17.1 0.0 copy-done.3
  17.2 0.0 copy-done.4
  17.2 0.0 copy-done.5
  17.2 7.6 %alone.1 = (f32[2,2,2048,256]{3,2,1,0:T(8,128)S(1)}, f32[2,2,16,128]{3,2,1,0:T(8,128)S(1)}, s32[4]{0:T(128)S(1)}, bf16[2,2,2048,128]{3,2,1,0:T(8,128)(2,1)S(1)},...) custom-call(s32[3]{0:T(128)S(1)} %pad_add_fusion.refs_0_, s32[8]{0:T(128)S(1)} %copy-done.4, ...), custom_call_target="tpu_custom_call" | custom-call | flops 15000000512 | bytes 262144 | tf_op jit(solution)/shard_map/alone/pallas_call | solution.py:458
  24.8 0.0 collective-permute-done.1.refs_7_.refs_11_
  24.8 3.3 %collective-permute-start.2 = (bf16[512,512]{1,0:T(8,128)(2,1)S(1)}, bf16[512,512]{1,0:T(8,128)(2,1)S(1)}, u32[]{:S(2)}, u32[]{:S(2)}) collective-permute-start(bf16[512,512]{1,0:T(8,128)(2,1)S(1)} %collective-permute-done.1.refs_7_.refs_11_), channel_id=1, source_target_pairs={{0,4},{1,5},{4,8},{5,9},{6,2},{7,3},{8,12},{9,13},{10,6},{11,7},{1... | collective-permute-start | bytes 1572872 | tf_op jit(solution)/shard_map/ppermute | solution.py:504
  28.1 2.1 collective-permute-start.3
  30.2 0.0 copy-done.1
  30.2 12.3 %near.1 = (f32[2,2,2048,256]{3,2,1,0:T(8,128)S(1)}, f32[2,2,16,128]{3,2,1,0:T(8,128)S(1)}) custom-call(s32[3]{0:T(128)S(1)} %pad_add_fusion.refs_0_, s32[4]{0:T(128)S(1)} %get-tuple-element.29.refs_1_, bf16[2,2,2048,128]{3,2,1,0:T(8,128)(2,1)S(1)} %get-tuple-element.30.refs_2_, ...), custom_call_target="tpu_custom_call", output_to_operand_aliasing={{0}: (7, {}), {1}: (8, {})} | custom-call | flops 10000000000 | bytes 262144 | tf_op jit(solution)/shard_map/near/pallas_call | solution.py:458
  42.5 0.0 collective-permute-done.6.refs_8_.refs_12_
  42.5 0.0 collective-permute-done.5.refs_5_.refs_6_.refs_9_.refs_10_
  42.5 0.0 collective-permute-done.7.refs_9_.refs_10_.refs_13_.refs_14_
  42.6 10.6 %middle.1 = (f32[2,2,2048,256]{3,2,1,0:T(8,128)S(1)}, f32[2,2,16,128]{3,2,1,0:T(8,128)S(1)}) custom-call(s32[3]{0:T(128)S(1)} %pad_add_fusion.refs_0_, s32[4]{0:T(128)S(1)} %get-tuple-element.29.refs_1_, bf16[2,2,2048,128]{3,2,1,0:T(8,128)(2,1)S(1)} %get-tuple-element.30.refs_2_, ...), custom_call_target="tpu_custom_call", output_to_operand_aliasing={{0}: (11, {}), {1}: (12, {})} | custom-call | flops 10000000000 | bytes 262144 | tf_op jit(solution)/shard_map/middle/pallas_call | solution.py:458
  53.2 0.0 collective-permute-done.2.refs_5_
  53.2 0.0 collective-permute-done.3.refs_6_
  53.2 99.6 %far.2 = (bf16[128,8192]{1,0:T(8,128)(2,1)}, bf16[128,2048]{1,0:T(8,128)(2,1)S(1)}, f32[2,2,2048,256]{3,2,1,0:T(8,128)S(1)}, f32[2,2,16,128]{3,2,1,0:T(8,128)S(1)}) custom-call(s32[3]{0:T(128)S(1)} %pad_add_fusion.refs_0_, s32[4]{0:T(128)S(1)} %get-tuple-element.29.refs_1_, ...), custom_call_target="tpu_custom_call", output_to_operand_aliasing={{2}: (15, {}), {3}: (16, {})} | custom-call | flops 10000000000 | bytes 262144 | tf_op jit(solution)/shard_map/far/pallas_call | solution.py:458
  152.8 0.3 collective-permute-start.8
  153.1 99.8 %far.3 = (bf16[128,8192]{1,0:T(8,128)(2,1)}, bf16[128,2048]{1,0:T(8,128)(2,1)S(1)}, f32[2,2,2048,256]{3,2,1,0:T(8,128)S(1)}, f32[2,2,16,128]{3,2,1,0:T(8,128)S(1)}) custom-call(s32[3]{0:T(128)S(1)} %pad_add_fusion.refs_0_, s32[4]{0:T(128)S(1)} %get-tuple-element.29.refs_1_, ...), custom_call_target="tpu_custom_call", output_to_operand_aliasing={{2}: (15, {}), {3}: (16, {}), {0}: (17, {})} | custom-call | flops 10000000000 | bytes 262144 | tf_op jit(solution)/shard_map/far/pallas_call | solution.py:458
  252.9 0.5 collective-permute-start.9
  253.5 0.0 collective-permute-done.8
  253.5 0.8 constant_dynamic-update-slice_fusion.3
  254.3 0.7 collective-permute-done.9
  255.0 0.8 constant_dynamic-update-slice_fusion.2
  (1 shorter events, 0.0 us)
Async XLA Ops:
  1.3 15.8 %copy-start = (bf16[128,8192]{1,0:T(8,128)(2,1)S(1)}, bf16[128,8192]{1,0:T(8,128)(2,1)}, u32[]{:S(2)}) copy-start(bf16[128,8192]{1,0:T(8,128)(2,1)} %refs_5_.1) | copy-start | bytes 6291460
  1.3 15.8 %copy-start.2 = (bf16[128,512]{1,0:T(8,128)(2,1)S(1)}, bf16[128,512]{1,0:T(8,128)(2,1)}, u32[]{:S(2)}) copy-start(bf16[128,512]{1,0:T(8,128)(2,1)} %refs_6_.1) | copy-start | bytes 393220
  1.3 15.8 %copy-start.3 = (bf16[128,512]{1,0:T(8,128)(2,1)S(1)}, bf16[128,512]{1,0:T(8,128)(2,1)}, u32[]{:S(2)}) copy-start(bf16[128,512]{1,0:T(8,128)(2,1)} %refs_7_.1) | copy-start | bytes 393220
  1.3 15.8 %copy-start.4 = (s32[8]{0:T(128)S(1)}, s32[8]{0:T(128)}, u32[]{:S(2)}) copy-start(s32[8]{0:T(128)} %refs_1_.1) | copy-start | bytes 100
  5.6 11.5 %collective-permute-start = (bf16[128,4736]{1,0:T(8,128)(2,1)}, bf16[128,4736]{1,0:T(8,128)(2,1)}, u32[]{:S(2)}, u32[]{:S(2)}) collective-permute-start(bf16[128,4736]{1,0:T(8,128)(2,1)} %get-tuple-element.28), channel_id=1, source_target_pairs={{0,1},{1,0},{2,3},{3,2},{4,5},{5,4},{6,7},{7,6},{8,9},{9,8},{10,11... | collective-permute-start | bytes 3637256 | tf_op jit(solution)/shard_map/ppermute | solution.py:504
  6.3 3.3 %collective-permute-start.4 = (bf16[512,512]{1,0:T(8,128)(2,1)}, bf16[512,512]{1,0:T(8,128)(2,1)S(1)}, u32[]{:S(2)}, u32[]{:S(2)}) collective-permute-start(bf16[512,512]{1,0:T(8,128)(2,1)} %get-tuple-element.38), channel_id=1, source_target_pairs={{0,1},{1,0},{2,3},{3,2},{4,5},{5,4},{6,7},{7,6},{8,9},{9,8},{10,11... | collective-permute-start | bytes 1572872 | tf_op jit(solution)/shard_map/ppermute | solution.py:504
  6.4 18.4 %collective-permute-start.1 = (bf16[512,512]{1,0:T(8,128)(2,1)}, bf16[512,512]{1,0:T(8,128)(2,1)S(1)}, u32[]{:S(2)}, u32[]{:S(2)}) collective-permute-start(bf16[512,512]{1,0:T(8,128)(2,1)} %get-tuple-element.35.refs_5_.refs_7_), channel_id=1, source_target_pairs={{0,2},{1,3},{2,0},{3,1},{4,6},{5,7},{6,4},{7,5},{8,10},{9,11},{10,... | collective-permute-start | bytes 1572872 | tf_op jit(solution)/shard_map/ppermute | solution.py:504
  7.6 7.5 %copy-start.6 = (bf16[512,512]{1,0:T(8,128)(2,1)S(1)}, bf16[512,512]{1,0:T(8,128)(2,1)}, u32[]{:S(2)}) copy-start(bf16[512,512]{1,0:T(8,128)(2,1)} %get-tuple-element.38) | copy-start | bytes 1572868
  7.6 9.5 %copy-start.5 = (f32[384,128]{1,0:T(8,128)S(1)}, f32[384,128]{1,0:T(8,128)}, u32[]{:S(2)}) copy-start(f32[384,128]{1,0:T(8,128)} %constant.26.clone.refs_4_) | copy-start | bytes 589828
  9.7 20.5 %copy-start.1 = (bf16[512,512]{1,0:T(8,128)(2,1)S(1)}, bf16[512,512]{1,0:T(8,128)(2,1)}, u32[]{:S(2)}) copy-start(bf16[512,512]{1,0:T(8,128)(2,1)} %get-tuple-element.35.refs_5_.refs_7_) | copy-start | bytes 1572868
  9.7 32.8 %collective-permute-start.5 = (bf16[1024,512]{1,0:T(8,128)(2,1)S(1)}, bf16[1024,512]{1,0:T(8,128)(2,1)S(1)}, u32[]{:S(2)}, u32[]{:S(2)}) collective-permute-start(bf16[1024,512]{1,0:T(8,128)(2,1)S(1)} %constant_dynamic-update-slice_fusion), channel_id=1, source_target_pairs={{0,4},{1,5},{2,6},{3,7},{4,8},{5,9},{6,10},{7,11},{8,12},{9,13},{1... | collective-permute-start | bytes 3145736 | tf_op jit(solution)/shard_map/ppermute | solution.py:504
  13.1 29.5 %collective-permute-start.7 = (bf16[1024,512]{1,0:T(8,128)(2,1)S(1)}, bf16[1024,512]{1,0:T(8,128)(2,1)S(1)}, u32[]{:S(2)}, u32[]{:S(2)}) collective-permute-start(bf16[1024,512]{1,0:T(8,128)(2,1)S(1)} %constant_dynamic-update-slice_fusion), channel_id=1, source_target_pairs={{4,0},{5,1},{6,2},{7,3},{8,4},{9,5},{10,6},{11,7},{12,8},{13,9},{1... | collective-permute-start | bytes 3145736 | tf_op jit(solution)/shard_map/ppermute | solution.py:504
  15.2 27.4 %collective-permute-start.6 = (bf16[512,512]{1,0:T(8,128)(2,1)S(1)}, bf16[512,512]{1,0:T(8,128)(2,1)S(1)}, u32[]{:S(2)}, u32[]{:S(2)}) collective-permute-start(bf16[512,512]{1,0:T(8,128)(2,1)S(1)} %copy-done.6), channel_id=1, source_target_pairs={{0,3},{1,2},{2,1},{3,0},{4,7},{5,6},{6,5},{7,4},{8,11},{9,10},{10,... | collective-permute-start | bytes 1572872 | tf_op jit(solution)/shard_map/ppermute | solution.py:504
  24.8 28.3 %collective-permute-start.2 = (bf16[512,512]{1,0:T(8,128)(2,1)S(1)}, bf16[512,512]{1,0:T(8,128)(2,1)S(1)}, u32[]{:S(2)}, u32[]{:S(2)}) collective-permute-start(bf16[512,512]{1,0:T(8,128)(2,1)S(1)} %collective-permute-done.1.refs_7_.refs_11_), channel_id=1, source_target_pairs={{0,4},{1,5},{4,8},{5,9},{6,2},{7,3},{8,12},{9,13},{10,6},{11,7},{1... | collective-permute-start | bytes 1572872 | tf_op jit(solution)/shard_map/ppermute | solution.py:504
  28.1 25.1 %collective-permute-start.3 = (bf16[512,512]{1,0:T(8,128)(2,1)S(1)}, bf16[512,512]{1,0:T(8,128)(2,1)S(1)}, u32[]{:S(2)}, u32[]{:S(2)}) collective-permute-start(bf16[512,512]{1,0:T(8,128)(2,1)S(1)} %copy-done.6), channel_id=1, source_target_pairs={{2,5},{3,4},{4,3},{5,2},{6,9},{7,8},{8,7},{9,6},{10,13},{11,12},{1... | collective-permute-start | bytes 1572872 | tf_op jit(solution)/shard_map/ppermute | solution.py:504
  152.8 100.7 %collective-permute-start.8 = (bf16[128,2048]{1,0:T(8,128)(2,1)S(1)}, bf16[128,2048]{1,0:T(8,128)(2,1)S(1)}, u32[]{:S(2)}, u32[]{:S(2)}) collective-permute-start(bf16[128,2048]{1,0:T(8,128)(2,1)S(1)} %get-tuple-element.49), channel_id=1, source_target_pairs={{0,1},{1,0},{2,3},{3,2},{4,5},{5,4},{6,7},{7,6},{8,9},{9,8},{10,11... | collective-permute-start | bytes 1572872 | tf_op jit(solution)/shard_map/ppermute | solution.py:504
  252.9 2.1 collective-permute-start.9
